TPU v7x, 256 devices: a whole 4x4x8 slice. The times are simulated.
256 devices in a mesh: row: 16 (over y_lo, x, core), col: 16 (over y_hi, z).
Axes of the slice: x: 4, y: 4 (y_hi: 2, y_lo: 2; y = y_hi * 2 + y_lo), z: 8, core: 2. Of those that a mesh axis runs over, the one named last changes fastest.
Arguments:
- pair_tensor: float32 [512, 512, 128], P('row', 'col'), may hold values from -6 to 6
- norm_in_gain: float32 [2, 128], replicated, may hold values from 0.5 to 1.5
- norm_in_bias: float32 [2, 128], replicated, may hold values from -3 to 3
- proj_weight: bfloat16 [2, 128, 512], replicated, may hold values from -0.5 to 0.5
- gate_weight: bfloat16 [2, 128, 128], replicated, may hold values from -0.5 to 0.5
- norm_out_gain: float32 [2, 128], replicated, may hold values from 0.5 to 1.5
- norm_out_bias: float32 [2, 128], replicated, may hold values from -3 to 3
- out_weight: bfloat16 [2, 128, 128], replicated, may hold values from -0.5 to 0.5
Outputs:
- pair_out: float32 [512, 512, 128], P('row', 'col')
All inputs are finite; a program needn't handle non-finite values.
Results may differ from a plain program's by a relative error of at most 0.0023.
Values may be sent and summed in bfloat16 or wider, within the bound.
No kernel may reach another device: no remote copies, remote signals or barrier semaphores. Data moves between devices by JAX's collectives and lax.ppermute only.
A program may use at most 64 MiB of HBM per device.

v0:
```python
import jax
import jax.numpy as jnp
from jax import lax
from jax.sharding import PartitionSpec as P


def from_root(value, axis, source):
    kept = jnp.where(lax.axis_index(axis) == source, value, 0).astype(value.dtype)
    return lax.psum(kept, axis)


def layer_norm(values, gain_vec, bias_vec):
    average = jnp.mean(values, axis=-1, keepdims=True)
    centered = values - average
    variance = jnp.mean(centered * centered, axis=-1, keepdims=True)
    return centered * lax.rsqrt(variance + 1e-05) * gain_vec + bias_vec


def operands(pair_tensor, layer, norm_in_gain, norm_in_bias, proj_weight, gate_weight):
    width = pair_tensor.shape[-1]
    normed = layer_norm(pair_tensor, norm_in_gain[layer], norm_in_bias[layer]).astype(jnp.bfloat16)
    projected = jnp.dot(normed, proj_weight[layer], preferred_element_type=jnp.float32)
    left_op = (jax.nn.sigmoid(projected[..., 0:width]) * projected[..., width : 2 * width]).astype(
        jnp.bfloat16
    )
    right_op = (
        jax.nn.sigmoid(projected[..., 2 * width : 3 * width])
        * projected[..., 3 * width : 4 * width]
    ).astype(jnp.bfloat16)
    gate_values = jax.nn.sigmoid(
        jnp.dot(normed, gate_weight[layer], preferred_element_type=jnp.float32)
    )
    return (left_op, right_op, gate_values)


def finish(pair_tensor, product, gate_values, layer, norm_out_gain, norm_out_bias, out_weight):
    normed_product = layer_norm(product, norm_out_gain[layer], norm_out_bias[layer]).astype(
        jnp.bfloat16
    )
    update = gate_values * jnp.dot(
        normed_product, out_weight[layer], preferred_element_type=jnp.float32
    )
    return pair_tensor + update


def local(
    pair_tensor,
    norm_in_gain,
    norm_in_bias,
    proj_weight,
    gate_weight,
    norm_out_gain,
    norm_out_bias,
    out_weight,
):
    row_count = lax.axis_size("row")
    col_count = lax.axis_size("col")
    fanout = row_count // col_count
    row_id = lax.axis_index("row")
    col_id = lax.axis_index("col")
    left_op, right_op, gate_values = operands(
        pair_tensor, 0, norm_in_gain, norm_in_bias, proj_weight, gate_weight
    )
    right_rows = lax.all_gather(right_op, "col", axis=1, tiled=True)
    pieces = from_root(right_rows, "row", col_id * fanout + 0)
    matched = pieces
    product = jnp.einsum(
        "ikc,jkc->ijc",
        lax.all_gather(left_op, "col", axis=1, tiled=True),
        matched,
        preferred_element_type=jnp.float32,
    )
    current = finish(pair_tensor, product, gate_values, 0, norm_out_gain, norm_out_bias, out_weight)
    left_op, right_op, gate_values = operands(
        current, 1, norm_in_gain, norm_in_bias, proj_weight, gate_weight
    )
    strip_cols = lax.all_gather(left_op, "row", axis=0, tiled=True)
    partner_in = from_root(strip_cols, "col", row_id // fanout)
    matched = partner_in
    product = jnp.einsum(
        "kic,kjc->ijc",
        matched,
        lax.all_gather(right_op, "row", axis=0, tiled=True),
        preferred_element_type=jnp.float32,
    )
    return finish(current, product, gate_values, 1, norm_out_gain, norm_out_bias, out_weight)


def solution(mesh):
    return jax.shard_map(
        local,
        mesh=mesh,
        in_specs=(P("row", "col", None), P(), P(), P(), P(), P(), P(), P()),
        out_specs=P("row", "col", None),
        check_vma=False,
    )
```

profile of v0, /device:TPU:1, one launch (start us, length us, event | category | flops | bytes accessed | tf_op | source)
XLA Modules:
  0.0 644.9 jit_solution(7790855588752400589)
XLA Ops:
  6.5 1.2 reduce_sum.72
  7.8 1.4 multiply_reduce_fusion.3
  9.2 0.8 slice_bitcast_fusion.2
  10.0 1.6 fusion.34
  11.6 1.1 fusion.16
  12.6 0.0 all-gather.5.cloned.1.call-update
  12.7 0.0 all-gather.7.cloned.1.call-start
  12.7 0.7 all-gather.7.cloned.1.call-update
  13.4 0.0 all-reduce.3.cloned.1.call-start
  13.5 105.1 %all-gather.5.cloned.1.call-done = bf16[32,512,128]{2,1,0:T(8,128)(2,1)} async-done(((bf16[32,32,128]{2,1,0:T(8,128)(2,1)}), bf16[32,512,128]{2,1,0:T(8,128)(2,1)}) %all-gather.5.cloned.1.call-update) | async-done | bytes 4194320 | tf_op jit(solution)/shard_map/all_gather | solution.py:64
  118.5 2.2 broadcast_select_fusion.1
  120.8 0.0 all-reduce.3.cloned.1.call-update
  120.8 0.0 all-gather.11.cloned.1.call-start
  120.8 0.6 copy-done.4
  121.4 0.0 copy-done.5
  121.4 0.4 copy-done
  121.8 1.3 fusion.5
  123.1 99.8 %all-gather.7.cloned.1.call-done = bf16[32,512,128]{2,1,0:T(8,128)(2,1)} async-done(((bf16[32,32,128]{2,1,0:T(8,128)(2,1)}), bf16[32,512,128]{2,1,0:T(8,128)(2,1)}) %all-gather.7.cloned.1.call-update) | async-done | bytes 4194320 | tf_op jit(solution)/shard_map/all_gather | solution.py:69
  222.9 8.0 %copy.44 = bf16[32,512,128]{1,0,2:T(8,128)(2,1)} copy(bf16[32,512,128]{2,1,0:T(8,128)(2,1)} %all-gather.7.cloned.1.call-done) | data formatting | bytes 8388608 | tf_op jit(solution)/shard_map/all_gather | solution.py:69
  230.8 128.5 %all-reduce.3.cloned.1.call-done = bf16[32,512,128]{2,1,0:T(8,128)(2,1)} async-done(((bf16[32,512,128]{2,1,0:T(8,128)(2,1)}), bf16[32,512,128]{2,1,0:T(8,128)(2,1)}) %all-reduce.3.cloned.1.call-update) | async-done | bytes 4194320 | tf_op jit(solution)/shard_map/psum | solution.py:9
  359.4 7.9 %copy.43 = bf16[32,512,128]{1,0,2:T(8,128)(2,1)} copy(bf16[32,512,128]{2,1,0:T(8,128)(2,1)} %all-reduce.3.cloned.1.call-done) | data formatting | bytes 8388608 | tf_op jit(solution)/shard_map/psum | solution.py:9
  367.3 4.7 bitcast_reduce_fusion.1
  372.0 1.4 copy.45
  373.5 0.1 copy.47
  373.5 0.4 multiply_reduce_fusion.2
  373.9 0.3 copy-done.1
  374.3 1.8 fusion.46
  376.0 0.4 multiply_reduce_fusion.1
  376.4 0.5 fusion.32
  376.9 1.1 fusion.8
  378.0 0.0 all-gather.11.cloned.1.call-update
  378.0 0.0 all-gather.9.cloned.1.call-start
  378.1 0.5 all-gather.9.cloned.1.call-update
  378.6 0.2 all-reduce.5.cloned.1.call-start
  378.9 41.1 %all-gather.11.cloned.1.call-done = bf16[512,32,128]{2,1,0:T(8,128)(2,1)} async-done(((bf16[32,32,128]{2,1,0:T(8,128)(2,1)}), bf16[512,32,128]{2,1,0:T(8,128)(2,1)}) %all-gather.11.cloned.1.call-update) | async-done | bytes 4194320 | tf_op jit(solution)/shard_map/all_gather | solution.py:77
  420.0 8.6 %copy.50 = bf16[512,32,128]{0,1,2:T(8,128)(2,1)} copy(bf16[512,32,128]{2,1,0:T(8,128)(2,1)} %all-gather.11.cloned.1.call-done) | data formatting | bytes 8388608 | tf_op jit(solution)/shard_map/all_gather | solution.py:77
  428.6 2.2 broadcast_select_fusion
  430.8 0.0 all-reduce.5.cloned.1.call-update
  430.9 0.8 copy-done.7
  431.7 1.3 fusion.2
  432.9 28.8 %all-gather.9.cloned.1.call-done = bf16[512,32,128]{2,1,0:T(8,128)(2,1)} async-done(((bf16[32,32,128]{2,1,0:T(8,128)(2,1)}), bf16[512,32,128]{2,1,0:T(8,128)(2,1)}) %all-gather.9.cloned.1.call-update) | async-done | bytes 4194320 | tf_op jit(solution)/shard_map/all_gather | solution.py:83
  461.7 8.5 %copy.51 = bf16[512,32,128]{0,1,2:T(8,128)(2,1)} copy(bf16[512,32,128]{2,1,0:T(8,128)(2,1)} %all-gather.9.cloned.1.call-done) | data formatting | bytes 8388608 | tf_op jit(solution)/shard_map/all_gather | solution.py:83
  470.2 158.9 %all-reduce.5.cloned.1.call-done = bf16[512,32,128]{0,1,2:T(8,128)(2,1)} async-done(((bf16[512,32,128]{0,1,2:T(8,128)(2,1)}), bf16[512,32,128]{0,1,2:T(8,128)(2,1)}) %all-reduce.5.cloned.1.call-update) | async-done | bytes 4194320 | tf_op jit(solution)/shard_map/psum | solution.py:9
  629.1 4.7 bitcast_reduce_fusion
  633.8 1.4 copy.52
  635.3 0.1 copy.54
  635.3 0.4 multiply_reduce_fusion
  635.8 2.3 fusion.7
  (21 shorter events, 0.1 us)
Async XLA Ops:
  6.5 112.0 %all-gather.5.cloned.1.call-start = ((), (), s32[]{:S(2)}) async-start(), calls=%async_computation | async-start | bytes 4456448 | tf_op jit(solution)/shard_map/all_gather | solution.py:64
  12.7 210.2 %all-gather.7.cloned.1.call-start = ((), (), s32[]{:S(2)}) async-start(), calls=%async_computation.2 | async-start | bytes 4456448 | tf_op jit(solution)/shard_map/all_gather | solution.py:69
  13.4 345.9 %all-reduce.3.cloned.1.call-start = ((), (), s32[]{:S(2)}) async-start(), calls=%async_computation.1 | async-start | bytes 8388608 | tf_op jit(solution)/shard_map/psum | solution.py:9
  120.7 0.7 copy-start.4
  120.8 0.7 copy-start.5
  120.8 1.1 copy-start
  120.8 1.1 copy-start.6
  120.8 299.2 %all-gather.11.cloned.1.call-start = ((), (), s32[]{:S(2)}) async-start(), calls=%async_computation.4 | async-start | bytes 4456448 | tf_op jit(solution)/shard_map/all_gather | solution.py:77
  367.3 7.0 %copy-start.3 = (bf16[2,128,128]{2,1,0:T(8,128)(2,1)S(1)}, bf16[2,128,128]{2,1,0:T(8,128)(2,1)}, u32[]{:S(2)}) copy-start(bf16[2,128,128]{2,1,0:T(8,128)(2,1)} %param.15) | copy-start | bytes 196612
  372.0 4.4 copy-start.2
  373.5 0.8 copy-start.1
  378.0 83.7 %all-gather.9.cloned.1.call-start = ((), (), s32[]{:S(2)}) async-start(), calls=%async_computation.3 | async-start | bytes 4456448 | tf_op jit(solution)/shard_map/all_gather | solution.py:83
  378.6 250.5 %all-reduce.5.cloned.1.call-start = ((), (), s32[]{:S(2)}) async-start(), calls=%async_computation.5 | async-start | bytes 8388608 | tf_op jit(solution)/shard_map/psum | solution.py:9
  430.8 0.8 copy-start.7
Sparse Core Ops, SparseCore 0:
  12.8 105.6 all-gather.4
  121.0 101.8 all-gather.6
  225.5 133.7 all-reduce.2
  378.2 41.7 all-gather.10
  421.7 39.9 all-gather.8
  464.2 164.8 all-reduce.4
where the time goes:
time: 654 us; the launch traced here: 645 us
  waiting for transfers between devices  563 us (86%)
  local copies, waits for them, and re-layouts  38.9 us (6%)
  matrix products  18 us (3%)
  between operations  13.6 us (2%)
  other arithmetic  10.5 us (2%)
    psum x2, waiting for transfers between devices, from_root(): return lax.psum(kept, axis)  287 us
    all_gather x1, waiting for transfers between devices, local(): right_rows = lax.all_gather(right_op, 'col', axis=1, tiled=True)  105 us
    all_gather x1, waiting for transfers between devices, local(): lax.all_gather(left_op, 'col', axis=1, tiled=True)  99.8 us
    all_gather x1, waiting for transfers between devices, local(): strip_cols = lax.all_gather(left_op, 'row', axis=0, tiled=True)  41.1 us
    all_gather x1, waiting for transfers between devices, local(): lax.all_gather(right_op, 'row', axis=0, tiled=True)  28.8 us
  transfers between devices with their start and end apart: 6, of which 6 were waited for; matrix products, arithmetic and copies ran while one was open for 5% of the time, Pallas kernels for 0%

commit v1 on v0

v1 whole, which is shorter than its diff:
```python
import functools

import jax
import jax.numpy as jnp
from jax import lax
from jax.experimental import pallas as pl
from jax.experimental.pallas import tpu as pltpu
from jax.sharding import Mesh, PartitionSpec as P

C = 128
EPS = 1e-05
VMEM_LIMIT = 48 * 1024 * 1024


def full(memory_space=pltpu.VMEM):
    return pl.BlockSpec(memory_space=memory_space)


def params():
    return pltpu.CompilerParams(vmem_limit_bytes=VMEM_LIMIT)


def norm_rows(x, gain_row, bias_row):
    centered = x - jnp.mean(x, axis=-1, keepdims=True)
    variance = jnp.mean(centered * centered, axis=-1, keepdims=True)
    return centered * lax.rsqrt(variance + EPS) * gain_row + bias_row


def dot(a, b, contract):
    return lax.dot_general(a, b, (contract, ((), ())), preferred_element_type=jnp.float32)


def emit_operands(layer, z, s, gain_in, bias_in, proj, gate_w, wide, gate_out):
    rows = z.reshape(256, C)
    normed = norm_rows(rows, gain_in[layer : layer + 1, :], bias_in[layer : layer + 1, :])
    normed = normed.astype(jnp.bfloat16)
    gate_out[s : s + 2] = jax.nn.sigmoid(dot(normed, gate_w[layer], ((1,), (0,)))).reshape(2, 128, C)
    projected = dot(proj[layer], normed, ((0,), (1,)))
    left = jax.nn.sigmoid(projected[0:C]) * projected[C : 2 * C]
    right = jax.nn.sigmoid(projected[2 * C : 3 * C]) * projected[3 * C : 4 * C]
    for t in range(2):
        wide[:, s + t, :] = left[:, 128 * t : 128 * t + 128]
        wide[:, 8 + s + t, :] = right[:, 128 * t : 128 * t + 128]


def first_kernel(z_ref, gain_in, bias_in, proj, gate_w, ops_ref, gate_ref, wide):
    for s in range(0, 8, 2):
        z = jnp.stack([z_ref[:, s], z_ref[:, s + 1]])
        emit_operands(0, z, s, gain_in, bias_in, proj, gate_w, wide, gate_ref)
    ops_ref[...] = wide[...].astype(jnp.bfloat16)


def finish_kernel(layer, y_ref, z_ref, gate_ref, gain_out, bias_out, out_w, *rest):
    if layer == 0:
        gain_in, bias_in, proj, gate_w, z_out, ops_ref, gate_out, y32, wide = rest
    else:
        z_out, y32 = rest
    y = y_ref[...].astype(jnp.float32)
    y32[...] = y
    average = jnp.mean(y, axis=0)
    centered = y - average[None]
    scale = lax.rsqrt(jnp.mean(centered * centered, axis=0) + EPS)
    gain = jnp.transpose(jnp.broadcast_to(gain_out[layer : layer + 1, :], (C, C)))
    bias = jnp.transpose(jnp.broadcast_to(bias_out[layer : layer + 1, :], (C, C)))
    weight = out_w[layer]
    for s in range(0, 8, 2):
        new = []
        for t in (s, s + 1):
            tile = y32[:, t, :]
            normed = (tile - average[t : t + 1]) * scale[t : t + 1] * gain + bias
            update = gate_ref[t] * dot(normed.astype(jnp.bfloat16), weight, ((0,), (0,)))
            value = z_ref[:, t] + update.reshape(4, 32, C)
            z_out[:, t] = value
            new.append(value)
        if layer == 0:
            emit_operands(1, jnp.stack(new), s, gain_in, bias_in, proj, gate_w, wide, gate_out)
    if layer == 0:
        ops_ref[...] = wide[...].astype(jnp.bfloat16)


def swap_groups(tiles):
    lane = lax.broadcasted_iota(jnp.int32, tiles[0].shape, 1)
    low = lane < 64
    even = (lane // 32) % 2 == 0
    t0, t1, t2, t3 = tiles
    u0 = jnp.where(low, t0, pltpu.roll(t2, 64, 1))
    u2 = jnp.where(low, pltpu.roll(t0, 64, 1), t2)
    u1 = jnp.where(low, t1, pltpu.roll(t3, 64, 1))
    u3 = jnp.where(low, pltpu.roll(t1, 64, 1), t3)
    v0 = jnp.where(even, u0, pltpu.roll(u1, 32, 1))
    v1 = jnp.where(even, pltpu.roll(u0, 96, 1), u1)
    v2 = jnp.where(even, u2, pltpu.roll(u3, 32, 1))
    v3 = jnp.where(even, pltpu.roll(u2, 96, 1), u3)
    return v0, v1, v2, v3


def write_back(product, b, y_ref):
    for d, tile in enumerate(swap_groups(product)):
        y_ref[:, 4 * b + d] = tile.reshape(8, 8, 128).astype(jnp.bfloat16)


def tile_of(ref, part, index):
    return ref[:, index, 8 * part : 8 * part + 8, :].astype(jnp.float32).reshape(64, 128)


def outgoing_kernel(core_ref, own, other, y_ref, left, right):
    core = core_ref[0]
    for b in range(4):
        lanes = slice(128 * b, 128 * b + 128)
        cols = range(4 * b, 4 * b + 4)
        for a, tile in enumerate(swap_groups([tile_of(own, 0, q) for q in cols])):
            left[64 * a : 64 * a + 64, lanes] = tile.astype(jnp.bfloat16)
        for ref, place in ((own, core), (other, 1 - core)):
            part = 1 if ref is own else 0
            for a, tile in enumerate(swap_groups([tile_of(ref, part, q) for q in cols])):
                right[:, place, 8 * a : 8 * a + 8, lanes] = tile.reshape(8, 8, 128)
    rows = right[...].reshape(512, 512).astype(jnp.bfloat16)
    product = dot(left[...], rows, ((1,), (1,)))
    for b in range(4):
        write_back([product[64 * a : 64 * a + 64, 128 * b : 128 * b + 128] for a in range(4)], b, y_ref)


def incoming_kernel(core_ref, own, other, y_ref, left, right):
    core = core_ref[0]
    for half, ref in enumerate((own, other)):
        for b in range(4):
            lanes = slice(128 * b, 128 * b + 128)
            for a, tile in enumerate(swap_groups([tile_of(ref, 1, q) for q in range(4 * b, 4 * b + 4)])):
                at = 256 * half + 64 * a
                right[at : at + 64, lanes] = tile.astype(jnp.bfloat16)
        for b in range(2):
            lanes = slice(128 * b, 128 * b + 128)
            picks = [tile_of(ref, 0, 2 * t + core) for t in range(4 * b, 4 * b + 4)]
            for a, tile in enumerate(swap_groups(picks)):
                at = 256 * half + 64 * a
                left[at : at + 64, lanes] = tile.astype(jnp.bfloat16)
    product = dot(left[...], right[...], ((0,), (0,)))
    product = product.reshape(8, 4, 8, 512)
    for b in range(4):
        parts = [product[:, a, :, 128 * b : 128 * b + 128].reshape(64, 128) for a in range(4)]
        write_back(parts, b, y_ref)


def triangle(kernel, core, own, other, left_shape, right_scratch):
    return pl.pallas_call(
        kernel,
        out_shape=jax.ShapeDtypeStruct((8, 16, 8, 128), jnp.bfloat16),
        in_specs=[full(pltpu.SMEM), full(), full()],
        out_specs=full(),
        scratch_shapes=[pltpu.VMEM(left_shape, jnp.bfloat16), right_scratch],
        compiler_params=params(),
    )(core, own, other)


def local(z, gain_in, bias_in, proj, gate_w, gain_out, bias_out, out_w):
    core = lax.axis_index("core").astype(jnp.int32).reshape(1)
    swap = ((0, 1), (1, 0))
    group = ("rh", "col")
    z4 = z.reshape(4, 8, 32, C)
    ops_shape = jax.ShapeDtypeStruct((C, 16, 128), jnp.bfloat16)
    gate_shape = jax.ShapeDtypeStruct((8, 128, C), jnp.float32)
    z_shape = jax.ShapeDtypeStruct((4, 8, 32, C), jnp.float32)
    wide = pltpu.VMEM((C, 16, 128), jnp.float32)
    y32 = pltpu.VMEM((C, 8, 128), jnp.float32)

    ops, gate = pl.pallas_call(
        first_kernel,
        out_shape=(ops_shape, gate_shape),
        in_specs=[full()] * 5,
        out_specs=(full(), full()),
        scratch_shapes=[wide],
        compiler_params=params(),
    )(z4, gain_in, bias_in, proj, gate_w)

    own = lax.all_to_all(ops, group, 0, 0, tiled=True).reshape(8, 16, 16, 128)
    other = lax.ppermute(own[:, :, 8:], "core", swap)
    y = triangle(outgoing_kernel, core, own, other, (256, 512), pltpu.VMEM((8, 2, 32, 512), jnp.float32))
    y = lax.all_to_all(y.reshape(C, 8, 128), group, 0, 0, tiled=True)

    z4, ops, gate = pl.pallas_call(
        functools.partial(finish_kernel, 0),
        out_shape=(z_shape, ops_shape, gate_shape),
        in_specs=[full()] * 10,
        out_specs=(full(), full(), full()),
        scratch_shapes=[y32, wide],
        compiler_params=params(),
    )(y, z4, gate, gain_out, bias_out, out_w, gain_in, bias_in, proj, gate_w)

    own = lax.all_to_all(ops, group, 0, 0, tiled=True).reshape(8, 16, 16, 128)
    other = lax.ppermute(own, "core", swap)
    y = triangle(incoming_kernel, core, own, other, (512, 256), pltpu.VMEM((512, 512), jnp.bfloat16))
    y = lax.all_to_all(y.reshape(C, 8, 128), group, 0, 0, tiled=True)

    out = pl.pallas_call(
        functools.partial(finish_kernel, 1),
        out_shape=z_shape,
        in_specs=[full()] * 6,
        out_specs=full(),
        scratch_shapes=[y32],
        compiler_params=params(),
    )(y, z4, gate, gain_out, bias_out, out_w)
    return out.reshape(32, 32, C)


def solution(mesh):
    fine = Mesh(mesh.devices.reshape(8, 2, 16), ("rh", "core", "col"))
    block = P(("rh", "core"), "col", None)
    return jax.shard_map(
        local,
        mesh=fine,
        in_specs=(block, P(), P(), P(), P(), P(), P(), P()),
        out_specs=block,
        check_vma=False,
    )
```

time: 654 us -> 122 us (0.19); the launches traced: 645 us -> 121 us
  waiting for transfers between devices: 563 us -> 2.7 us
  blocking collectives: 0 us -> 99 us
  local copies, waits for them, and re-layouts: 38.9 us -> 4.9 us
  matrix products: 18 us -> 0 us
  between operations: 13.6 us -> 0.09 us
  other arithmetic: 10.5 us -> 0 us
  Pallas kernels: 0 us -> 8.67 us
    psum x2 -> x0, waiting for transfers between devices: 287 us -> none  [from_root(): return lax.psum(kept, axis)]
    all_gather x4 -> x0, waiting for transfers between devices: 275 us -> none  [the longest x1 105 us: local(): right_rows = lax.all_gather(right_op, 'col', axis=1, tiled=True)]
    all_to_all x0 -> x4, blocking collectives: none -> 99 us  [the longest x2 59.6 us: local(): own = lax.all_to_all(ops, group, 0, 0, tiled=True).reshape(8, 16, 16, 128)]
    all_gather x3 -> x0, local copies, waits for them, and re-layouts: 25.1 us -> none  [the longest x1 8.62 us: local(): strip_cols = lax.all_gather(left_op, 'row', axis=0, tiled=True)]
    dot_general x8 -> x0, matrix products: 18 us -> none  [the longest x1 4.72 us: local(): jnp.einsum('ikc,jkc->ijc', lax.all_gather(left_op, 'col', axis=1, tiled=T...]
    pallas_call x0 -> x5, Pallas kernels: none -> 8.67 us  [the longest x2 3.43 us: triangle(): pl.pallas_call(kernel, out_shape=jax.ShapeDtypeStruct((8, 16, 8, 128), jn...]
    psum x1 -> x0, local copies, waits for them, and re-layouts: 7.94 us -> none  [from_root(): return lax.psum(kept, axis)]
  transfers between devices with their start and end apart: 6 -> 2, of which waited for: 6 -> 2; matrix products, arithmetic and copies ran while one was open for 5% -> 0% of each run, Pallas kernels for 0% -> 0%
where the time goes in v1:
time: 122 us; the launch traced here: 121 us
  blocking collectives  99 us (81%)
  Pallas kernels  8.67 us (7%)
  starting transfers between devices  5.88 us (5%)
  local copies, waits for them, and re-layouts  4.9 us (4%)
  waiting for transfers between devices  2.7 us (2%)
    all_to_all x2, blocking collectives, local(): own = lax.all_to_all(ops, group, 0, 0, tiled=True).reshape(8, 16, 16, 128)  59.6 us
    all_to_all x2, blocking collectives, local(): y = lax.all_to_all(y.reshape(C, 8, 128), group, 0, 0, tiled=True)  39.4 us
    unnamed x24, local copies, waits for them, and re-layouts  4.85 us
    pallas_call x2, Pallas kernels, triangle(): pl.pallas_call(kernel, out_shape=jax.ShapeDtypeStruct((8, 16, 8, 128), jn...  3.43 us
    ppermute x1, starting transfers between devices, local(): other = lax.ppermute(own, 'core', swap)  3.12 us
    ppermute x1, starting transfers between devices, local(): other = lax.ppermute(own[:, :, 8:], 'core', swap)  2.76 us
  transfers between devices with their start and end apart: 2, of which 2 were waited for; matrix products, arithmetic and copies ran while one was open for 0% of the time, Pallas kernels for 0%

profile of v1, /device:TPU:1, one launch (start us, length us, event | category | flops | bytes accessed | tf_op | source)
XLA Modules:
  0.0 121.2 jit_solution(11168672154609554119)
XLA Ops:
  0.0 0.0 copy-start.7
  0.0 0.7 copy-done.7
  0.7 0.0 copy-start
  0.7 1.0 copy-done
  1.7 0.0 copy-start.2
  1.7 0.9 copy-done.2
  2.7 0.0 copy-start.5
  2.7 0.8 copy-done.5
  3.5 0.0 copy-start.8
  3.5 0.7 copy-done.8
  4.2 1.3 %shard_map.82 = (bf16[128,16,128]{2,1,0:T(8,128)(2,1)S(1)}, f32[8,128,128]{2,1,0:T(8,128)S(1)}) custom-call(f32[4,8,32,128]{3,2,1,0:T(8,128)S(1)} %bitcast.11, f32[2,128]{1,0:T(2,128)S(1)} %copy-done.7, f32[2,128]{1,0:T(2,128)S(1)} %copy-done.8, bf16[2,128,512]{2,1,0:T(8,128)(2,1)S(1)} %copy-done.2, bf16[2,128,128]{2,1,0:T(8,128)(2,1)S(1)} %copy-done.5), custom_call_target="tpu_custom_call" | custom-call | tf_op jit(solution)/shard_map/pallas_call | solution.py:166
  5.5 35.1 %all_to_all.20 = bf16[128,16,128]{2,1,0:T(8,128)(2,1)S(1)} all-to-all(bf16[128,16,128]{2,1,0:T(8,128)(2,1)S(1)} %get-tuple-element.10), channel_id=1, replica_groups=mesh['rh'=8,'core'=2,'col'=16] {'rh','col'}, dimensions={0} | all-to-all | bytes 1048576 | tf_op jit(solution)/shard_map/all_to_all | solution.py:175
  40.7 2.8 %collective-permute-start = (bf16[8,16,8,128]{3,2,1,0:T(8,128)(2,1)S(1)}, bf16[8,16,8,128]{3,2,1,0:T(8,128)(2,1)S(1)}, u32[]{:S(2)}, u32[]{:S(2)}) collective-permute-start(bf16[8,16,8,128]{3,2,1,0:T(8,128)(2,1)S(1)} %slice.4), channel_id=1, source_target_pairs={{0,16},{16,0},{1,17},{17,1},{2,18},{18,2},{3,19},{19,3},{4,20},{20... | collective-permute-start | bytes 786440 | tf_op jit(solution)/shard_map/ppermute | solution.py:176
  43.5 1.2 collective-permute-done.other
  44.6 0.0 copy-start.3
  44.6 0.0 copy-start.4
  44.6 0.0 copy-start.6
  44.6 1.6 %shard_map.83 = bf16[8,16,8,128]{3,2,1,0:T(8,128)(2,1)S(1)} custom-call(s32[1]{0:T(128)} %bitcast.core_ref, bf16[8,16,16,128]{3,2,1,0:T(8,128)(2,1)S(1)} %bitcast.8, bf16[8,16,8,128]{3,2,1,0:T(8,128)(2,1)S(1)} %collective-permute-done.other), custom_call_target="tpu_custom_call" | custom-call | tf_op jit(solution)/shard_map/pallas_call | solution.py:145
  46.2 0.0 copy-start.1
  46.2 0.0 copy-start.10
  46.2 0.0 copy-start.11
  46.2 19.8 %all_to_all.21.y_ref = bf16[128,8,128]{2,1,0:T(8,128)(2,1)S(1)} all-to-all(bf16[128,8,128]{2,1,0:T(8,128)(2,1)S(1)} %bitcast.14), channel_id=1, replica_groups=mesh['rh'=8,'core'=2,'col'=16] {'rh','col'}, dimensions={0} | all-to-all | bytes 524288 | tf_op jit(solution)/shard_map/all_to_all | solution.py:178
  66.0 0.0 copy-start.9
  66.0 0.0 copy-done.3
  66.0 0.0 copy-done.4
  66.0 0.0 copy-done.6
  66.0 0.0 copy-done.1
  66.0 0.0 copy-done.10
  66.0 0.0 copy-done.11
  66.0 0.6 copy-done.9
  66.7 2.3 %shard_map.84 = (f32[4,8,32,128]{3,2,1,0:T(8,128)S(1)}, bf16[128,16,128]{2,1,0:T(8,128)(2,1)S(1)}, f32[8,128,128]{2,1,0:T(8,128)S(1)}) custom-call(bf16[128,8,128]{2,1,0:T(8,128)(2,1)S(1)} %all_to_all.21.y_ref, f32[4,8,32,128]{3,2,1,0:T(8,128)S(1)} %bitcast.12, f32[8,128,128]{2,1,0:T(8,128)S(1)} %get-tuple-element.11.gate_ref, f32[2,128]{1,0:T(2,128)S(1)} %copy-done.10, ...), custom_call_target="tpu_custom_call" | custom-call | tf_op jit(solution)/shard_map/pallas_call | solution.py:180
  69.0 24.5 %all_to_all.22 = bf16[128,16,128]{2,1,0:T(8,128)(2,1)S(1)} all-to-all(bf16[128,16,128]{2,1,0:T(8,128)(2,1)S(1)} %get-tuple-element.12), channel_id=1, replica_groups=mesh['rh'=8,'core'=2,'col'=16] {'rh','col'}, dimensions={0} | all-to-all | bytes 1048576 | tf_op jit(solution)/shard_map/all_to_all | solution.py:189
  93.5 3.1 %collective-permute-start.1 = (bf16[8,16,16,128]{3,2,1,0:T(8,128)(2,1)S(1)}, bf16[8,16,16,128]{3,2,1,0:T(8,128)(2,1)S(1)}, u32[]{:S(2)}, u32[]{:S(2)}) collective-permute-start(bf16[8,16,16,128]{3,2,1,0:T(8,128)(2,1)S(1)} %bitcast.9), channel_id=1, source_target_pairs={{0,16},{16,0},{1,17},{17,1},{2,18},{18,2},{3,19},{19,3},{4,20},{20... | collective-permute-start | bytes 1572872 | tf_op jit(solution)/shard_map/ppermute | solution.py:190
  96.6 1.5 %collective-permute-done.1.other = bf16[8,16,16,128]{3,2,1,0:T(8,128)(2,1)S(1)} collective-permute-done((bf16[8,16,16,128]{3,2,1,0:T(8,128)(2,1)S(1)}, bf16[8,16,16,128]{3,2,1,0:T(8,128)(2,1)S(1)}, u32[]{:S(2)}, u32[]{:S(2)}) %collective-permute-start.1) | collective-permute-done | bytes 524320 | tf_op jit(solution)/shard_map/ppermute | solution.py:190
  98.1 1.9 %shard_map.85 = bf16[8,16,8,128]{3,2,1,0:T(8,128)(2,1)S(1)} custom-call(s32[1]{0:T(128)} %bitcast.core_ref, bf16[8,16,16,128]{3,2,1,0:T(8,128)(2,1)S(1)} %bitcast.10, bf16[8,16,16,128]{3,2,1,0:T(8,128)(2,1)S(1)} %collective-permute-done.1.other), custom_call_target="tpu_custom_call" | custom-call | tf_op jit(solution)/shard_map/pallas_call | solution.py:145
  100.0 19.6 %all_to_all.23.y_ref = bf16[128,8,128]{2,1,0:T(8,128)(2,1)S(1)} all-to-all(bf16[128,8,128]{2,1,0:T(8,128)(2,1)S(1)} %bitcast.13), channel_id=1, replica_groups=mesh['rh'=8,'core'=2,'col'=16] {'rh','col'}, dimensions={0} | all-to-all | bytes 524288 | tf_op jit(solution)/shard_map/all_to_all | solution.py:192
  119.7 1.6 %shard_map.86 = f32[4,8,32,128]{3,2,1,0:T(8,128)} custom-call(bf16[128,8,128]{2,1,0:T(8,128)(2,1)S(1)} %all_to_all.23.y_ref, f32[4,8,32,128]{3,2,1,0:T(8,128)S(1)} %get-tuple-element.13.z_ref, f32[8,128,128]{2,1,0:T(8,128)S(1)} %get-tuple-element.14.gate_ref, f32[2,128]{1,0:T(2,128)S(1)} %copy-done.10, f32[2,128]{1,0:T(2,128)S(1)} %copy-done.11, ...), custom_call_target="tpu_custom_call" | custom-call | tf_op jit(solution)/shard_map/pallas_call | solution.py:194
  (1 shorter events, 0.0 us)
Async XLA Ops:
  0.0 0.7 copy-start.7
  0.7 1.0 copy-start
  1.7 0.9 copy-start.2
  2.7 0.8 copy-start.5
  3.5 0.7 copy-start.8
  40.7 3.9 %collective-permute-start = (bf16[8,16,8,128]{3,2,1,0:T(8,128)(2,1)S(1)}, bf16[8,16,8,128]{3,2,1,0:T(8,128)(2,1)S(1)}, u32[]{:S(2)}, u32[]{:S(2)}) collective-permute-start(bf16[8,16,8,128]{3,2,1,0:T(8,128)(2,1)S(1)} %slice.4), channel_id=1, source_target_pairs={{0,16},{16,0},{1,17},{17,1},{2,18},{18,2},{3,19},{19,3},{4,20},{20... | collective-permute-start | bytes 786440 | tf_op jit(solution)/shard_map/ppermute | solution.py:176
  44.6 21.4 %copy-start.3 = (bf16[2,128,512]{2,1,0:T(8,128)(2,1)S(1)}, bf16[2,128,512]{2,1,0:T(8,128)(2,1)}, u32[]{:S(2)}) copy-start(bf16[2,128,512]{2,1,0:T(8,128)(2,1)} %rest_2_.1) | copy-start | bytes 786436
  44.6 21.4 %copy-start.4 = (bf16[2,128,128]{2,1,0:T(8,128)(2,1)S(1)}, bf16[2,128,128]{2,1,0:T(8,128)(2,1)}, u32[]{:S(2)}) copy-start(bf16[2,128,128]{2,1,0:T(8,128)(2,1)} %out_w.3) | copy-start | bytes 196612
  44.6 21.4 %copy-start.6 = (bf16[2,128,128]{2,1,0:T(8,128)(2,1)S(1)}, bf16[2,128,128]{2,1,0:T(8,128)(2,1)}, u32[]{:S(2)}) copy-start(bf16[2,128,128]{2,1,0:T(8,128)(2,1)} %rest_3_.1) | copy-start | bytes 196612
  46.2 19.8 %copy-start.1 = (f32[32,32,128]{2,1,0:T(8,128)S(1)}, f32[32,32,128]{2,1,0:T(8,128)}, u32[]{:S(2)}) copy-start(f32[32,32,128]{2,1,0:T(8,128)} %param.8) | copy-start | bytes 1572868
  46.2 19.8 %copy-start.10 = (f32[2,128]{1,0:T(2,128)S(1)}, f32[2,128]{1,0:T(2,128)}, u32[]{:S(2)}) copy-start(f32[2,128]{1,0:T(2,128)} %gain_out.3) | copy-start | bytes 3076
  46.2 19.8 %copy-start.11 = (f32[2,128]{1,0:T(2,128)S(1)}, f32[2,128]{1,0:T(2,128)}, u32[]{:S(2)}) copy-start(f32[2,128]{1,0:T(2,128)} %bias_out.3) | copy-start | bytes 3076
  66.0 0.7 copy-start.9
  93.5 4.7 %collective-permute-start.1 = (bf16[8,16,16,128]{3,2,1,0:T(8,128)(2,1)S(1)}, bf16[8,16,16,128]{3,2,1,0:T(8,128)(2,1)S(1)}, u32[]{:S(2)}, u32[]{:S(2)}) collective-permute-start(bf16[8,16,16,128]{3,2,1,0:T(8,128)(2,1)S(1)} %bitcast.9), channel_id=1, source_target_pairs={{0,16},{16,0},{1,17},{17,1},{2,18},{18,2},{3,19},{19,3},{4,20},{20... | collective-permute-start | bytes 1572872 | tf_op jit(solution)/shard_map/ppermute | solution.py:190
